TPU v7x, 128 devices: a whole 4x4x4 slice. The times are simulated.
128 devices in a mesh: lat: 8 (over y, core), lon: 16 (over x, z).
Axes of the slice: x: 4, y: 4, z: 4, core: 2. Of those that a mesh axis runs over, the one named last changes fastest.
Arguments:
- grid_feats: bfloat16 [65536, 474], P(('lat', 'lon')), may hold values from -6 to 6
- mesh_latent: bfloat16 [65536, 512], P(('lat', 'lon')), may hold values from -6 to 6
- embed_in: bfloat16 [474, 512], replicated, may hold values from -0.25 to 0.25
- embed_out: bfloat16 [512, 512], replicated, may hold values from -0.25 to 0.25
- enc_send: bfloat16 [512, 512], replicated, may hold values from -0.25 to 0.25
- enc_recv: bfloat16 [512, 512], replicated, may hold values from -0.25 to 0.25
- enc_edge_out: bfloat16 [512, 512], replicated, may hold values from -0.25 to 0.25
- enc_node_self: bfloat16 [512, 512], replicated, may hold values from -0.25 to 0.25
- enc_node_agg: bfloat16 [512, 512], replicated, may hold values from -0.25 to 0.25
- enc_node_out: bfloat16 [512, 512], replicated, may hold values from -0.25 to 0.25
- proc_send: bfloat16 [512, 512], replicated, may hold values from -0.25 to 0.25
- proc_recv: bfloat16 [512, 512], replicated, may hold values from -0.25 to 0.25
- proc_edge_out: bfloat16 [512, 512], replicated, may hold values from -0.25 to 0.25
- proc_node_self: bfloat16 [512, 512], replicated, may hold values from -0.25 to 0.25
- proc_node_agg: bfloat16 [512, 512], replicated, may hold values from -0.25 to 0.25
- proc_node_out: bfloat16 [512, 512], replicated, may hold values from -0.25 to 0.25
- dest_dev: int32 [65536, 2], P(('lat', 'lon')), may hold values from 0 to 127, all different within a row; in each aligned block of 512 rows (0 to 511, 512 to 1023, ...) at most 16 rows name the same one
- dest_node: int32 [65536, 2], P(('lat', 'lon')), may hold values from 0 to 511
- send_rows: int32 [128, 128, 4], P(('lat', 'lon')), may hold values from 0 to 511
- src_slot: int32 [65536, 8], P(('lat', 'lon')), may hold values from 0 to 1023
Outputs:
- mesh_out: bfloat16 [65536, 512], P(('lat', 'lon'))
Inputs may be any that keep to these rules, and one draw needn't show every extreme that they name: `dest_dev`: in the rows of one device, no device is named more than 16 times and some device exactly 16 times; a row's two devices differ.
All inputs are finite; a program needn't handle non-finite values.
Results may differ from a plain program's by a relative error of at most 0.017.
Values may be sent and summed in bfloat16 or wider, within the bound.
A program may use at most 64 MiB of HBM per device.

v0:
```python
import jax
import jax.numpy as jnp
from jax import lax
from jax.sharding import PartitionSpec as P


def swish_act(values):
    return values * jax.nn.sigmoid(values)


def embed_rows(features, embed_in, embed_out):
    hidden = swish_act(jnp.dot(features, embed_in, preferred_element_type=jnp.float32)).astype(
        jnp.bfloat16
    )
    return jnp.dot(hidden, embed_out, preferred_element_type=jnp.float32).astype(jnp.bfloat16)


def node_update(latent, summed, w_self, w_agg, w_out):
    preact = jnp.dot(latent, w_self, preferred_element_type=jnp.float32) + jnp.dot(
        summed, w_agg, preferred_element_type=jnp.float32
    )
    hidden = swish_act(preact).astype(jnp.bfloat16)
    return (
        latent.astype(jnp.float32) + jnp.dot(hidden, w_out, preferred_element_type=jnp.float32)
    ).astype(jnp.bfloat16)


def slot_ranks(flat_dest, peer_count):
    edge_count = flat_dest.shape[0]
    block_rows = min(512, edge_count)
    onehot = (flat_dest[:, None] == jnp.arange(peer_count, dtype=jnp.int32)[None, :]).astype(
        jnp.bfloat16
    )
    onehot = onehot.reshape(edge_count // block_rows, block_rows, peer_count)
    strict_lower = (jnp.arange(block_rows)[:, None] > jnp.arange(block_rows)[None, :]).astype(
        jnp.bfloat16
    )
    within = jnp.einsum("ij,bjp->bip", strict_lower, onehot, preferred_element_type=jnp.float32)
    totals = jnp.sum(onehot, axis=1, dtype=jnp.float32)
    offsets = jnp.cumsum(totals, axis=0) - totals
    counted = jnp.sum((within + offsets[:, None, :]) * onehot, axis=2)
    return counted.reshape(edge_count).astype(jnp.int32)


def on_device(
    grid_feats,
    mesh_latent,
    embed_in,
    embed_out,
    enc_send,
    enc_recv,
    enc_edge_out,
    enc_node_self,
    enc_node_agg,
    enc_node_out,
    proc_send,
    proc_recv,
    proc_edge_out,
    proc_node_self,
    proc_node_agg,
    proc_node_out,
    dest_dev,
    dest_node,
    send_rows,
    src_slot,
):
    lat_count = lax.axis_size("lat")
    lon_count = lax.axis_size("lon")
    peer_count = lat_count * lon_count
    row_count = grid_feats.shape[0]
    node_count = mesh_latent.shape[0]
    latent_width = mesh_latent.shape[1]
    capacity = max(2, 4 * row_count // peer_count)
    slot_total = peer_count * capacity
    slot_block = min(512, slot_total)
    flat_dest = dest_dev.reshape(-1)
    position = (flat_dest * capacity + slot_ranks(flat_dest, peer_count)).reshape(row_count, 2)
    outgoing_rows = embed_rows(grid_feats, embed_in, embed_out)

    def fill_block(start):
        columns = start + jnp.arange(slot_block, dtype=jnp.int32)
        hits = position[:, :, None] == columns[None, None, :]
        pick = jnp.any(hits, axis=1).astype(jnp.bfloat16)
        rows_block = jnp.einsum(
            "rs,rc->sc", pick, outgoing_rows, preferred_element_type=jnp.float32
        ).astype(jnp.bfloat16)
        node_ids = jnp.sum(jnp.where(hits, dest_node[:, :, None], 0), axis=(0, 1))
        filled = jnp.any(hits, axis=(0, 1))
        return (rows_block, jnp.where(filled, node_ids, node_count))

    block_starts = jnp.arange(slot_total // slot_block, dtype=jnp.int32) * slot_block
    payload_blocks, target_blocks = lax.map(fill_block, block_starts)
    payload = payload_blocks.reshape(slot_total, -1)
    targets = target_blocks.reshape(slot_total)
    node_ids_all = jnp.arange(node_count, dtype=jnp.int32)
    rows_in = lax.all_to_all(
        payload.reshape(peer_count, capacity, -1),
        ("lat", "lon"),
        split_axis=0,
        concat_axis=0,
        tiled=True,
    )
    targets_in = lax.all_to_all(
        targets.reshape(peer_count, capacity),
        ("lat", "lon"),
        split_axis=0,
        concat_axis=0,
        tiled=True,
    )
    flat_rows = rows_in.reshape(-1, rows_in.shape[-1])
    pick = (targets_in.reshape(-1)[:, None] == node_ids_all[None, :]).astype(jnp.bfloat16)
    recv_rows = jnp.dot(pick, mesh_latent, preferred_element_type=jnp.float32).astype(jnp.bfloat16)
    preact = jnp.dot(flat_rows, enc_send, preferred_element_type=jnp.float32) + jnp.dot(
        recv_rows, enc_recv, preferred_element_type=jnp.float32
    )
    hidden = swish_act(preact).astype(jnp.bfloat16)
    messages = jnp.dot(hidden, enc_edge_out, preferred_element_type=jnp.float32)
    messages, arrived = (
        messages.reshape(rows_in.shape[0], rows_in.shape[1], latent_width),
        targets_in,
    )
    spread = (node_ids_all[:, None] == arrived.reshape(-1)[None, :]).astype(jnp.float32)
    summed = jnp.dot(
        spread,
        messages.reshape(-1, latent_width),
        precision=lax.Precision.HIGHEST,
        preferred_element_type=jnp.float32,
    )
    mesh_one = node_update(
        mesh_latent, summed.astype(jnp.bfloat16), enc_node_self, enc_node_agg, enc_node_out
    )
    halo_count = send_rows.shape[2]
    chooser = (send_rows.reshape(-1)[:, None] == node_ids_all[None, :]).astype(jnp.bfloat16)
    outgoing = jnp.dot(chooser, mesh_one, preferred_element_type=jnp.float32).astype(jnp.bfloat16)
    incoming = lax.all_to_all(
        outgoing.reshape(peer_count, halo_count, latent_width),
        ("lat", "lon"),
        split_axis=0,
        concat_axis=0,
        tiled=True,
    )
    sender_table = jnp.concatenate([mesh_one, incoming.reshape(-1, latent_width)], axis=0)
    table_ids = jnp.arange(sender_table.shape[0], dtype=jnp.int32)
    flat_slots = src_slot.reshape(-1)
    edge_block = min(512, flat_slots.shape[0])

    def gather_block(slots):
        pick = (slots[:, None] == table_ids[None, :]).astype(jnp.bfloat16)
        return jnp.dot(pick, sender_table, preferred_element_type=jnp.float32).astype(jnp.bfloat16)

    gathered = lax.map(gather_block, flat_slots.reshape(-1, edge_block)).reshape(-1, latent_width)
    degree = src_slot.shape[1]
    recv_two = jnp.dot(mesh_one, proc_recv, preferred_element_type=jnp.float32)
    preact = (
        jnp.dot(gathered, proc_send, preferred_element_type=jnp.float32).reshape(
            node_count, degree, latent_width
        )
        + recv_two[:, None, :]
    )
    hidden = swish_act(preact).astype(jnp.bfloat16).reshape(-1, latent_width)
    messages_two = jnp.dot(hidden, proc_edge_out, preferred_element_type=jnp.float32).reshape(
        node_count, degree, latent_width
    )
    summed_two = jnp.sum(messages_two, axis=1).astype(jnp.bfloat16)
    return node_update(mesh_one, summed_two, proc_node_self, proc_node_agg, proc_node_out)


def solution(mesh):
    in_specs = (
        P(("lat", "lon"), None),
        P(("lat", "lon"), None),
        P(),
        P(),
        P(),
        P(),
        P(),
        P(),
        P(),
        P(),
        P(),
        P(),
        P(),
        P(),
        P(),
        P(),
        P(("lat", "lon"), None),
        P(("lat", "lon"), None),
        P(("lat", "lon"), None, None),
        P(("lat", "lon"), None),
    )
    out_specs = P(("lat", "lon"), None)
    return jax.shard_map(
        on_device, mesh=mesh, in_specs=in_specs, out_specs=out_specs, check_vma=False
    )
```

profile of v0, /device:TPU:1, one launch (start us, length us, event | category | flops | bytes accessed | tf_op | source)
XLA Modules:
  0.0 157.1 jit_solution(10919398251558774044)
XLA Ops:
  0.0 0.9 copy.40
  0.9 0.7 broadcast_multiply_fusion
  1.6 0.2 eq.89
  1.8 0.1 convert_reduce_fusion
  1.9 0.4 fusion.30
  2.4 0.1 copy.39
  2.5 0.2 mul.32
  2.7 3.0 %convolution_convert_fusion.2 = bf16[512,512]{1,0:T(8,128)(2,1)} fusion(bf16[512,512]{1,0:T(8,128)(2,1)} %param.27, bf16[512,474]{0,1:T(8,128)(2,1)} %param.24, bf16[474,512]{1,0:T(8,128)(2,1)} %param.26), kind=kOutput, calls=%fused_computation.38 | convolution fusion | flops 518520832 | bytes 2019328 | tf_op jit(solution)/shard_map/dot_general | solution.py:15
  5.7 16.6 %while.23 = (s32[]{:T(128)}, bf16[4,512,512]{2,1,0:T(8,128)(2,1)S(1)}, s32[4,512]{1,0:T(4,128)S(1)}, s32[1024]{0:T(1024)S(1)}, s32[4]{0:T(128)S(1)}, /*index=5*/...) while((s32[]{:T(128)}, bf16[4,512,512]{2,1,0:T(8,128)(2,1)S(1)}, ...), condition=%wide.region_7.8_spmd, body=%wide.region_3.7_spmd.sunk | while | flops 271581184 | bytes 1619061 | solution.py:92
  5.7 0.7 dynamic_slice.12
  6.4 0.7 iota_add_fusion.2
  7.1 0.2 eq.197
  7.4 0.4 compare_reduce_fusion.3
  7.8 0.4 fusion.88
  8.3 1.5 fusion.87
  9.9 0.7 dynamic_slice.12
  10.5 0.7 iota_add_fusion.2
  11.2 0.2 eq.197
  11.5 0.4 compare_reduce_fusion.3
  11.9 0.4 fusion.88
  12.4 1.5 fusion.87
  14.0 0.7 dynamic_slice.12
  14.7 0.7 iota_add_fusion.2
  15.4 0.2 eq.197
  15.7 0.4 compare_reduce_fusion.3
  16.1 0.4 fusion.88
  16.6 1.5 fusion.87
  18.1 0.7 dynamic_slice.12
  18.8 0.7 iota_add_fusion.2
  19.5 0.2 eq.197
  19.8 0.4 compare_reduce_fusion.3
  20.2 0.4 fusion.88
  20.7 1.5 fusion.87
  22.4 20.8 %all_to_all.19 = s32[128,1,16]{2,1,0:T(1,128)S(1)} all-to-all(s32[128,1,16]{2,1,0:T(1,128)S(1)} %bitcast.77), channel_id=1, replica_groups=mesh['lat'=8,'lon'=16] {'lat','lon'}, dimensions={0} | all-to-all | bytes 16384 | tf_op jit(solution)/shard_map/all_to_all | solution.py:103
  43.2 4.5 %all-to-all-start.1 = ((bf16[128,16,512]{2,1,0:T(8,128)(2,1)}), bf16[128,16,512]{2,1,0:T(8,128)(2,1)S(1)}, u32[]{:S(2)}, u32[]{:S(2)}) async-start(bf16[128,16,512]{2,1,0:T(8,128)(2,1)} %bitcast.76), calls=%async_computation.1 | async-start | bytes 4194304 | tf_op jit(solution)/shard_map/all_to_all | solution.py:96
  48.2 0.2 reshape_reshape.8
  48.3 2.5 %fusion.49 = f32[512,512]{1,0:T(8,128)} fusion(bf16[512,512]{1,0:T(8,128)(2,1)} %param.25, bf16[512,512]{1,0:T(8,128)(2,1)S(1)} %copy-done.5), kind=kOutput, calls=%fused_computation.71 | convolution fusion | flops 268435456 | bytes 2097152 | tf_op jit(solution)/shard_map/dot_general | solution.py:19
  50.8 0.5 broadcast.65
  51.3 0.9 reduce.3
  52.3 3.6 %fusion.16 = bf16[2048,512]{1,0:T(8,128)(2,1)} fusion(bf16[512,512]{1,0:T(8,128)(2,1)} %param.25, s32[2048]{0:T(1024)S(1)} %eq.93), kind=kOutput, calls=%fused_computation.27 | convolution fusion | flops 1075838976 | bytes 2629632 | tf_op jit(solution)/shard_map/dot_general | solution.py:112
  55.8 21.7 %all-to-all-done.1 = bf16[128,16,512]{2,1,0:T(8,128)(2,1)S(1)} async-done(((bf16[128,16,512]{2,1,0:T(8,128)(2,1)}), bf16[128,16,512]{2,1,0:T(8,128)(2,1)S(1)}, u32[]{:S(2)}, u32[]{:S(2)}) %all-to-all-start.1) | async-done | bytes 2097184 | tf_op jit(solution)/shard_map/all_to_all | solution.py:96
  77.5 3.2 %fusion.50 = f32[2048,512]{1,0:T(8,128)} fusion(bf16[2048,512]{1,0:T(8,128)(2,1)S(1)} %bitcast.75, bf16[512,512]{1,0:T(8,128)(2,1)S(1)} %copy-done.4), kind=kOutput, calls=%fused_computation.72 | convolution fusion | flops 1073741824 | bytes 6815744 | tf_op jit(solution)/shard_map/dot_general | solution.py:113
  80.7 7.8 %fusion.24 = f32[2048,512]{1,0:T(8,128)} fusion(bf16[512,512]{1,0:T(8,128)(2,1)} %param.30, f32[2048,512]{1,0:T(8,128)} %fusion.50, bf16[2048,512]{1,0:T(8,128)(2,1)} %fusion.16, bf16[512,512]{1,0:T(8,128)(2,1)} %param.29), kind=kOutput, calls=%fused_computation.31 | convolution fusion | flops 2153775104 | bytes 11534336 | tf_op jit(solution)/shard_map/dot_general | solution.py:117
  88.5 6.9 %fusion.25 = bf16[512,512]{1,0:T(8,128)(2,1)} fusion(f32[2048,512]{1,0:T(8,128)} %fusion.24, s32[2048]{0:T(1024)S(1)} %eq.93), kind=kOutput, calls=%fused_computation.36 | convolution fusion | flops 6443761664 | bytes 4726784 | tf_op jit(solution)/shard_map/dot_general | solution.py:123
  95.5 2.3 %fusion.26 = bf16[512,512]{1,0:T(8,128)(2,1)S(1)} fusion(bf16[512,512]{1,0:T(8,128)(2,1)} %param.33, f32[512,512]{1,0:T(8,128)S(1)} %copy-done.3, bf16[512,512]{1,0:T(8,128)(2,1)} %fusion.25, bf16[512,512]{1,0:T(8,128)(2,1)} %param.32, bf16[512,512]{1,0:T(8,128)(2,1)S(1)} %copy-done.6), kind=kOutput, calls=%fused_computation.39 | convolution fusion | flops 539230208 | bytes 3670016 | tf_op jit(solution)/shard_map/dot_general | solution.py:24
  97.7 0.5 convolution_convert_fusion.1
  98.2 0.9 reshape.81
  99.1 4.7 %all-to-all-start.2 = ((bf16[128,4,512]{2,1,0:T(4,128)(2,1)}), bf16[128,4,512]{2,1,0:T(4,128)(2,1)S(1)}, u32[]{:S(2)}, u32[]{:S(2)}) async-start(bf16[128,4,512]{2,1,0:T(4,128)(2,1)} %reshape.81), calls=%async_computation.2 | async-start | bytes 1048576 | tf_op jit(solution)/shard_map/all_to_all | solution.py:135
  103.8 1.4 fusion.52
  105.2 1.5 fusion.51
  106.7 10.5 %all-to-all-done.2 = bf16[128,4,512]{2,1,0:T(4,128)(2,1)S(1)} async-done(((bf16[128,4,512]{2,1,0:T(4,128)(2,1)}), bf16[128,4,512]{2,1,0:T(4,128)(2,1)S(1)}, u32[]{:S(2)}, u32[]{:S(2)}) %all-to-all-start.2) | async-done | bytes 524320 | tf_op jit(solution)/shard_map/all_to_all | solution.py:135
  117.4 1.1 pad_maximum_fusion
  118.5 22.4 %while.24 = (s32[]{:T(128)}, bf16[8,512,512]{2,1,0:T(8,128)(2,1)}, s32[8,512]{1,0:T(8,128)S(1)}, bf16[1024,512]{1,0:T(8,128)(2,1)}, s32[]{:T(128)}) while((s32[]{:T(128)}, bf16[8,512,512]{2,1,0:T(8,128)(2,1)}, s32[8,512]{1,0:T(8,128)S(1)}, bf16[1024,512]{1,0:T(8,128)(2,1)}, s32[]{:T(128)}) %tuple.40), condition=%wide.region_9.10_spmd.clone, body=%wide.region_8.9_spmd.clone.sunk | while | flops 537657344 | bytes 1579585 | solution.py:151
  118.5 2.9 %fusion.90 = bf16[8,512,512]{2,1,0:T(8,128)(2,1)} fusion(bf16[8,512,512]{2,1,0:T(8,128)(2,1)} %get-tuple-element.212, s32[]{:T(128)} %get-tuple-element.211, bf16[1024,512]{1,0:T(8,128)(2,1)} %get-tuple-element.219, s32[512]{0:T(512)S(1)} %bitcast.79), kind=kOutput, calls=%fused_computation.14.clone.1 | convolution fusion | flops 537657344 | bytes 1575424 | tf_op jit(solution)/shard_map/while/body/eval_jaxpr/dot_general | solution.py:149
  121.3 2.8 %fusion.90 = bf16[8,512,512]{2,1,0:T(8,128)(2,1)} fusion(bf16[8,512,512]{2,1,0:T(8,128)(2,1)} %get-tuple-element.212, s32[]{:T(128)} %get-tuple-element.211, bf16[1024,512]{1,0:T(8,128)(2,1)} %get-tuple-element.219, s32[512]{0:T(512)S(1)} %bitcast.79), kind=kOutput, calls=%fused_computation.14.clone.1 | convolution fusion | flops 537657344 | bytes 1575424 | tf_op jit(solution)/shard_map/while/body/eval_jaxpr/dot_general | solution.py:149
  124.1 2.8 %fusion.90 = bf16[8,512,512]{2,1,0:T(8,128)(2,1)} fusion(bf16[8,512,512]{2,1,0:T(8,128)(2,1)} %get-tuple-element.212, s32[]{:T(128)} %get-tuple-element.211, bf16[1024,512]{1,0:T(8,128)(2,1)} %get-tuple-element.219, s32[512]{0:T(512)S(1)} %bitcast.79), kind=kOutput, calls=%fused_computation.14.clone.1 | convolution fusion | flops 537657344 | bytes 1575424 | tf_op jit(solution)/shard_map/while/body/eval_jaxpr/dot_general | solution.py:149
  126.9 2.8 %fusion.90 = bf16[8,512,512]{2,1,0:T(8,128)(2,1)} fusion(bf16[8,512,512]{2,1,0:T(8,128)(2,1)} %get-tuple-element.212, s32[]{:T(128)} %get-tuple-element.211, bf16[1024,512]{1,0:T(8,128)(2,1)} %get-tuple-element.219, s32[512]{0:T(512)S(1)} %bitcast.79), kind=kOutput, calls=%fused_computation.14.clone.1 | convolution fusion | flops 537657344 | bytes 1575424 | tf_op jit(solution)/shard_map/while/body/eval_jaxpr/dot_general | solution.py:149
  129.7 2.8 %fusion.90 = bf16[8,512,512]{2,1,0:T(8,128)(2,1)} fusion(bf16[8,512,512]{2,1,0:T(8,128)(2,1)} %get-tuple-element.212, s32[]{:T(128)} %get-tuple-element.211, bf16[1024,512]{1,0:T(8,128)(2,1)} %get-tuple-element.219, s32[512]{0:T(512)S(1)} %bitcast.79), kind=kOutput, calls=%fused_computation.14.clone.1 | convolution fusion | flops 537657344 | bytes 1575424 | tf_op jit(solution)/shard_map/while/body/eval_jaxpr/dot_general | solution.py:149
  132.5 2.8 %fusion.90 = bf16[8,512,512]{2,1,0:T(8,128)(2,1)} fusion(bf16[8,512,512]{2,1,0:T(8,128)(2,1)} %get-tuple-element.212, s32[]{:T(128)} %get-tuple-element.211, bf16[1024,512]{1,0:T(8,128)(2,1)} %get-tuple-element.219, s32[512]{0:T(512)S(1)} %bitcast.79), kind=kOutput, calls=%fused_computation.14.clone.1 | convolution fusion | flops 537657344 | bytes 1575424 | tf_op jit(solution)/shard_map/while/body/eval_jaxpr/dot_general | solution.py:149
  135.3 2.8 %fusion.90 = bf16[8,512,512]{2,1,0:T(8,128)(2,1)} fusion(bf16[8,512,512]{2,1,0:T(8,128)(2,1)} %get-tuple-element.212, s32[]{:T(128)} %get-tuple-element.211, bf16[1024,512]{1,0:T(8,128)(2,1)} %get-tuple-element.219, s32[512]{0:T(512)S(1)} %bitcast.79), kind=kOutput, calls=%fused_computation.14.clone.1 | convolution fusion | flops 537657344 | bytes 1575424 | tf_op jit(solution)/shard_map/while/body/eval_jaxpr/dot_general | solution.py:149
  138.1 2.8 %fusion.90 = bf16[8,512,512]{2,1,0:T(8,128)(2,1)} fusion(bf16[8,512,512]{2,1,0:T(8,128)(2,1)} %get-tuple-element.212, s32[]{:T(128)} %get-tuple-element.211, bf16[1024,512]{1,0:T(8,128)(2,1)} %get-tuple-element.219, s32[512]{0:T(512)S(1)} %bitcast.79), kind=kOutput, calls=%fused_computation.14.clone.1 | convolution fusion | flops 537657344 | bytes 1575424 | tf_op jit(solution)/shard_map/while/body/eval_jaxpr/dot_general | solution.py:149
  140.9 8.0 %multiply_convert_fusion = bf16[512,8,512]{2,0,1:T(8,128)(2,1)S(1)} fusion(f32[512,512]{1,0:T(8,128)S(1)} %copy-done.2, bf16[512,8,512]{2,1,0:T(8,128)(2,1)} %bitcast.81, bf16[512,512]{1,0:T(8,128)(2,1)S(1)} %copy-done), kind=kOutput, calls=%fused_computation.17 | convolution fusion | flops 2160066560 | bytes 9961472 | tf_op jit(solution)/shard_map/dot_general | solution.py:155
  149.0 5.4 %fusion.17 = bf16[512,512]{1,0:T(8,128)(2,1)} fusion(bf16[512,8,512]{2,0,1:T(8,128)(2,1)S(1)} %multiply_convert_fusion, bf16[512,512]{1,0:T(8,128)(2,1)S(1)} %copy-done.11), kind=kOutput, calls=%fused_computation.28 | convolution fusion | flops 2149318656 | bytes 5242880 | tf_op jit(solution)/shard_map/dot_general | solution.py:161
  154.4 2.7 %fusion.27 = bf16[512,512]{1,0:T(8,128)(2,1)} fusion(bf16[512,512]{1,0:T(8,128)(2,1)S(1)} %copy-done.12, f32[512,512]{1,0:T(8,128)S(1)} %fusion.51, bf16[512,512]{1,0:T(8,128)(2,1)S(1)} %copy-done.13, bf16[512,512]{1,0:T(8,128)(2,1)S(1)} %fusion.26, bf16[512,512]{1,0:T(8,128)(2,1)} %fusion.17), kind=kOutput, calls=%fused_computation.40 | convolution fusion | flops 539230208 | bytes 3670016 | tf_op jit(solution)/shard_map/dot_general | solution.py:24
  (63 shorter events, 1.5 us)
Async XLA Ops:
  0.0 140.9 %copy-start = (bf16[512,512]{1,0:T(8,128)(2,1)S(1)}, bf16[512,512]{1,0:T(8,128)(2,1)}, u32[]{:S(2)}) copy-start(bf16[512,512]{1,0:T(8,128)(2,1)} %param.34) | copy-start | bytes 1572868
  2.3 3.4 %copy-start.8 = (s32[512,2]{0,1:T(2,128)S(1)}, s32[512,2]{0,1:T(2,128)}, u32[]{:S(2)}) copy-start(s32[512,2]{0,1:T(2,128)} %param.41) | copy-start | bytes 12292
  22.3 21.0 %copy-start.1 = (bf16[4,512,512]{2,1,0:T(8,128)(2,1)}, bf16[4,512,512]{2,1,0:T(8,128)(2,1)S(1)}, u32[]{:S(2)}) copy-start(bf16[4,512,512]{2,1,0:T(8,128)(2,1)S(1)} %get-tuple-element.71) | copy-start | bytes 6291460
  22.3 25.5 %copy-start.10 = (s32[1,128,4]{1,2,0:T(4,128)S(1)}, s32[1,128,4]{1,2,0:T(4,128)}, u32[]{:S(2)}) copy-start(s32[1,128,4]{1,2,0:T(4,128)} %param.42) | copy-start | bytes 6148
  22.3 25.7 %copy-start.9 = (s32[512,8]{0,1:T(8,128)S(1)}, s32[512,8]{0,1:T(8,128)}, u32[]{:S(2)}) copy-start(s32[512,8]{0,1:T(8,128)} %param.43) | copy-start | bytes 49156
  22.3 26.0 %copy-start.5 = (bf16[512,512]{1,0:T(8,128)(2,1)S(1)}, bf16[512,512]{1,0:T(8,128)(2,1)}, u32[]{:S(2)}) copy-start(bf16[512,512]{1,0:T(8,128)(2,1)} %param.31) | copy-start | bytes 1572868
  43.2 34.3 %all-to-all-start.1 = ((bf16[128,16,512]{2,1,0:T(8,128)(2,1)}), bf16[128,16,512]{2,1,0:T(8,128)(2,1)S(1)}, u32[]{:S(2)}, u32[]{:S(2)}) async-start(bf16[128,16,512]{2,1,0:T(8,128)(2,1)} %bitcast.76), calls=%async_computation.1 | async-start | bytes 4194304 | tf_op jit(solution)/shard_map/all_to_all | solution.py:96
  51.3 26.2 %copy-start.4 = (bf16[512,512]{1,0:T(8,128)(2,1)S(1)}, bf16[512,512]{1,0:T(8,128)(2,1)}, u32[]{:S(2)}) copy-start(bf16[512,512]{1,0:T(8,128)(2,1)} %param.28) | copy-start | bytes 1572868
  88.5 6.9 %copy-start.3 = (f32[512,512]{1,0:T(8,128)S(1)}, f32[512,512]{1,0:T(8,128)}, u32[]{:S(2)}) copy-start(f32[512,512]{1,0:T(8,128)} %fusion.49) | copy-start | bytes 3145732
  88.5 6.9 %copy-start.6 = (bf16[512,512]{1,0:T(8,128)(2,1)S(1)}, bf16[512,512]{1,0:T(8,128)(2,1)}, u32[]{:S(2)}) copy-start(bf16[512,512]{1,0:T(8,128)(2,1)} %param.25) | copy-start | bytes 1572868
  95.5 8.4 %copy-start.7 = (bf16[512,512]{1,0:T(8,128)(2,1)S(1)}, bf16[512,512]{1,0:T(8,128)(2,1)}, u32[]{:S(2)}) copy-start(bf16[512,512]{1,0:T(8,128)(2,1)} %param.35) | copy-start | bytes 1572868
  99.1 18.1 %all-to-all-start.2 = ((bf16[128,4,512]{2,1,0:T(4,128)(2,1)}), bf16[128,4,512]{2,1,0:T(4,128)(2,1)S(1)}, u32[]{:S(2)}, u32[]{:S(2)}) async-start(bf16[128,4,512]{2,1,0:T(4,128)(2,1)} %reshape.81), calls=%async_computation.2 | async-start | bytes 1048576 | tf_op jit(solution)/shard_map/all_to_all | solution.py:135
  118.5 22.4 %copy-start.2 = (f32[512,512]{1,0:T(8,128)S(1)}, f32[512,512]{1,0:T(8,128)}, u32[]{:S(2)}) copy-start(f32[512,512]{1,0:T(8,128)} %fusion.52) | copy-start | bytes 3145732
  140.9 8.0 %copy-start.11 = (bf16[512,512]{1,0:T(8,128)(2,1)S(1)}, bf16[512,512]{1,0:T(8,128)(2,1)}, u32[]{:S(2)}) copy-start(bf16[512,512]{1,0:T(8,128)(2,1)} %param.36) | copy-start | bytes 1572868
  148.9 5.4 %copy-start.12 = (bf16[512,512]{1,0:T(8,128)(2,1)S(1)}, bf16[512,512]{1,0:T(8,128)(2,1)}, u32[]{:S(2)}) copy-start(bf16[512,512]{1,0:T(8,128)(2,1)} %param.39) | copy-start | bytes 1572868
  149.0 5.4 %copy-start.13 = (bf16[512,512]{1,0:T(8,128)(2,1)S(1)}, bf16[512,512]{1,0:T(8,128)(2,1)}, u32[]{:S(2)}) copy-start(bf16[512,512]{1,0:T(8,128)(2,1)} %param.38) | copy-start | bytes 1572868
where the time goes:
time: 158 us; the launch traced here: 157 us
  matrix products  77.6 us (49%)
  waiting for transfers between devices  32.2 us (20%)
  blocking collectives  20.8 us (13%)
  starting transfers between devices  9.21 us (6%)
  other arithmetic  8.99 us (6%)
  local copies, waits for them, and re-layouts  7.79 us (5%)
    dot_general x8, matrix products, gather_block(): jnp.dot(pick, sender_table, preferred_element_type=jnp.float32)  22.4 us
    all_to_all x1, waiting for transfers between devices, on_device(): lax.all_to_all(payload.reshape(peer_count, capacity, -1), ('lat', 'lon'),...  21.7 us
    all_to_all x1, blocking collectives, on_device(): lax.all_to_all(targets.reshape(peer_count, capacity), ('lat', 'lon'), spl...  20.8 us
    all_to_all x1, waiting for transfers between devices, on_device(): lax.all_to_all(outgoing.reshape(peer_count, halo_count, latent_width), ('...  10.5 us
    dot_general x1, matrix products, on_device(): jnp.dot(gathered, proc_send, preferred_element_type=jnp.float32)  8.02 us
    dot_general x1, matrix products, on_device(): messages = jnp.dot(hidden, enc_edge_out, preferred_element_type=jnp.float32)  7.81 us
    dot_general x1, matrix products, on_device(): jnp.dot(spread, messages.reshape(-1, latent_width), precision=lax.Precisi...  6.93 us
    dot_general x4, matrix products, fill_block(): jnp.einsum('rs,rc->sc', pick, outgoing_rows, preferred_element_type=jnp.f...  6.11 us
  transfers between devices with their start and end apart: 2, of which 2 were waited for; matrix products, arithmetic and copies ran while one was open for 7% of the time, Pallas kernels for 0%

commit v1 on v0

v1 whole, which is shorter than its diff:
```python
import functools

import jax
import jax.numpy as jnp
from jax import lax
from jax.experimental import pallas as pl
from jax.experimental.pallas import tpu as pltpu
from jax.sharding import PartitionSpec as P

MESH = pl.DeviceIdType.MESH
BF16 = jnp.bfloat16
F32 = jnp.float32
PEERS = 128
CAP = 16
HALO = 4
GROUP = 16
GROUPS = PEERS // GROUP
DIM = 512
CHANNELS = 474
ROWS = 512
TAIL = CHANNELS // 16 * 16
DEGREE = 8

(
    EMBED_OUT,
    ENC_SEND,
    ENC_RECV,
    ENC_EDGE_OUT,
    ENC_NODE_SELF,
    ENC_NODE_AGG,
    ENC_NODE_OUT,
    PROC_SEND,
    PROC_RECV,
    PROC_EDGE_OUT,
    PROC_NODE_SELF,
    PROC_NODE_AGG,
    PROC_NODE_OUT,
) = range(13)


def ring_distance(step):
    return min(step, 4 - step)


OFFSETS = sorted(
    (
        (dy, dc, dx, dz)
        for dy in range(4)
        for dc in range(2)
        for dx in range(4)
        for dz in range(4)
        if (dy, dc, dx, dz) != (0, 0, 0, 0)
    ),
    key=lambda o: -(ring_distance(o[0]) + ring_distance(o[2]) + ring_distance(o[3]) + 0.1 * o[1]),
)


def swish(values):
    return values * (0.5 * jnp.tanh(0.5 * values) + 0.5)


def dot(left, right):
    return jnp.dot(left, right, preferred_element_type=F32)


def dot_nt(left, right):
    return lax.dot_general(left, right, (((1,), (1,)), ((), ())), preferred_element_type=F32)


def dot_tn(left, right):
    return lax.dot_general(left, right, (((0,), (0,)), ((), ())), preferred_element_type=F32)


def iota(shape, dimension):
    return lax.broadcasted_iota(jnp.int32, shape, dimension)


def kernel(
    feats_hbm,
    latent_hbm,
    embed_in_hbm,
    *rest,
):
    weights_hbm = rest[:13]
    (dest_hbm, node_hbm, send_rows_hbm, slot_hbm, out_ref) = rest[13:18]
    (
        feats,
        aug,
        latent,
        embed_raw,
        embed_in,
        weights,
        dest,
        node,
        send_rows,
        slot,
        outgoing,
        arriving,
        halo_out,
        halo_in,
        recv_proj,
        self_part,
        fold_enc,
        fold_proc,
        spread,
        hidden_sum,
        chooser,
        pick_local,
        pick_halo,
        mesh_one,
        projected,
        receiver,
        local_part,
        load_sem,
        weight_sem,
        send_sem,
        recv_sem,
        halo_send_sem,
        halo_recv_sem,
        own_sem,
    ) = rest[18:]

    lat, lon = lax.axis_index("lat"), lax.axis_index("lon")
    me = lat * 16 + lon
    lats = {(dy, dc): ((lat // 2 + dy) % 4) * 2 + (lat + dc) % 2 for dy in range(4) for dc in range(2)}
    lons = {(dx, dz): ((lon // 4 + dx) % 4) * 4 + (lon + dz) % 4 for dx in range(4) for dz in range(4)}

    def peer(offset):
        dy, dc, dx, dz = offset
        return lats[dy, dc], lons[dx, dz]

    loads = [
        pltpu.make_async_copy(source, target, load_sem.at[i])
        for i, (source, target) in enumerate(
            (
                (dest_hbm, dest),
                (node_hbm, node),
                (feats_hbm, feats),
                (latent_hbm, latent),
                (embed_in_hbm, embed_raw),
                (send_rows_hbm, send_rows),
                (slot_hbm, slot),
            )
        )
    ]
    weight_loads = [
        pltpu.make_async_copy(source, weights.at[i], weight_sem.at[i])
        for i, source in enumerate(weights_hbm)
    ]
    for load in loads:
        load.start()

    barrier = pltpu.get_barrier_semaphore()
    for offset in OFFSETS:
        pl.semaphore_signal(barrier, inc=1, device_id=peer(offset), device_id_type=MESH)
    for load in weight_loads:
        load.start()

    loads[0].wait()
    loads[1].wait()
    dests = dest[...]
    nodes = node[...]
    owner = iota((PEERS, ROWS), 0)
    hits = [dests[k : k + 1, :] == owner for k in range(2)]
    onehot = jnp.concatenate([jnp.where(hit, 1.0, 0.0).astype(BF16) for hit in hits], axis=0)
    earlier = jnp.where(iota((ROWS, ROWS), 0) < iota((ROWS, ROWS), 1), 1.0, 0.0).astype(BF16)
    ranks = dot(onehot, earlier)
    first_count = jnp.sum(jnp.where(hits[0], 1.0, 0.0), axis=1, keepdims=True)
    start = owner.astype(F32) * CAP
    positions = [
        jnp.sum(jnp.where(hits[0], ranks[:PEERS] + start, 0.0), axis=0, keepdims=True),
        jnp.sum(jnp.where(hits[1], ranks[PEERS:] + first_count + start, 0.0), axis=0, keepdims=True),
    ]
    positions = [p.astype(jnp.int32) for p in positions]

    loads[2].wait()
    aug[0:TAIL, :] = feats[0:TAIL, :]
    meta = [dests[0:1] + 1, nodes[0:1] // 32, nodes[0:1] % 32, dests[1:2] + 1, nodes[1:2] // 32, nodes[1:2] % 32]
    left = CHANNELS - TAIL
    tail = jnp.concatenate(
        [feats[TAIL:CHANNELS, :].astype(F32), jnp.zeros((16 - left, ROWS), F32)], axis=0
    )
    tail_row = iota((16, ROWS), 0)
    for i, value in enumerate(meta):
        tail = jnp.where(tail_row == left + i, value.astype(F32), tail)
    aug[TAIL : TAIL + 16, :] = tail.astype(BF16)
    aug[TAIL + 16 :, :] = jnp.zeros((DIM - TAIL - 16, ROWS), BF16)

    def pack(block, carry):
        slots = iota((512, ROWS), 0) + block * 512
        pick = jnp.where((positions[0] == slots) | (positions[1] == slots), 1.0, 0.0).astype(BF16)
        rows = dot_nt(pick, aug[...]).astype(BF16)
        outgoing[pl.ds(block * 32, 32)] = rows.reshape(32, CAP, DIM)
        return carry

    lax.fori_loop(0, PEERS * CAP // 512, pack, 0)

    pl.semaphore_wait(barrier, PEERS - 1)
    for step, offset in enumerate(OFFSETS):
        to_lat, to_lon = peer(offset)
        pltpu.make_async_remote_copy(
            src_ref=outgoing.at[to_lat * 16 + to_lon],
            dst_ref=arriving.at[step],
            send_sem=send_sem,
            recv_sem=recv_sem.at[step // GROUP],
            device_id=(to_lat, to_lon),
            device_id_type=MESH,
        ).start()
    own = pltpu.make_async_copy(outgoing.at[me], arriving.at[PEERS - 1], own_sem)
    own.start()

    loads[4].wait()
    embed_in[0:TAIL, :] = embed_raw[0:TAIL, :]
    embed_tail = jnp.concatenate(
        [embed_raw[TAIL:CHANNELS, :].astype(F32), jnp.zeros((16 - left, DIM), F32)], axis=0
    )
    embed_in[TAIL : TAIL + 16, :] = embed_tail.astype(BF16)
    embed_in[TAIL + 16 :, :] = jnp.zeros((DIM - TAIL - 16, DIM), BF16)
    loads[3].wait()
    for load in weight_loads:
        load.wait()
    recv_proj[...] = dot(latent[...], weights[ENC_RECV]).astype(BF16)
    hidden_sum[...] = jnp.zeros((ROWS, DIM), F32)
    lane = iota((128, 2 * DIM), 0) - (CHANNELS - (DIM - 128))
    right = jnp.where(iota((128, 2 * DIM), 1) >= DIM, 3, 0)
    lane = lane - right
    spread[...] = jnp.where(
        lane == 0, 512.0, jnp.where(lane == 1, 32.0, jnp.where(lane == 2, 1.0, 0.0))
    ).astype(BF16)
    self_part[...] = dot(latent[...], weights[ENC_NODE_SELF])
    fold_enc[...] = dot(weights[ENC_EDGE_OUT], weights[ENC_NODE_AGG]).astype(BF16)
    fold_proc[...] = dot(weights[PROC_EDGE_OUT], weights[PROC_NODE_AGG]).astype(BF16)

    loads[5].wait()
    loads[6].wait()
    chosen = send_rows[0]
    chosen = jnp.concatenate([chosen // 32, chosen % 32], axis=0).astype(F32).astype(BF16)
    repeat = jnp.where(iota((PEERS * HALO, PEERS), 0) // HALO == iota((PEERS * HALO, PEERS), 1), 1.0, 0.0)
    chosen = dot_nt(repeat.astype(BF16), chosen)
    column = iota((PEERS * HALO, 2 * HALO), 1)
    chosen = jnp.where(column < HALO, chosen * 32.0, chosen)
    mine = column % HALO == iota((PEERS * HALO, 2 * HALO), 0) % HALO
    chosen = jnp.sum(jnp.where(mine, chosen, 0.0), axis=1, keepdims=True).astype(jnp.int32)
    node_lane = iota((ROWS, ROWS), 1)
    chooser[...] = jnp.where(chosen == node_lane, 1.0, 0.0).astype(BF16)

    slots = slot[...]
    slots = jnp.concatenate([slots // 32, slots % 32], axis=0).astype(F32).astype(BF16)
    identity = jnp.where(iota((ROWS, ROWS), 0) == node_lane, 1.0, 0.0).astype(BF16)
    slots = dot_nt(identity, slots)
    slots = (slots[:, :DEGREE] * 32.0 + slots[:, DEGREE:]).astype(jnp.int32)
    for k in range(DEGREE):
        wanted = slots[:, k : k + 1]
        pick_local[k] = jnp.where(wanted == node_lane, 1.0, 0.0).astype(BF16)
        pick_halo[k] = jnp.where(wanted - ROWS == node_lane, 1.0, 0.0).astype(BF16)

    def arrive(group):
        rows = arriving[pl.ds(group * GROUP, GROUP)].reshape(GROUP * CAP, DIM)
        embedded = swish(dot(rows, embed_in[...])).astype(BF16)
        grid_latent = dot(embedded, weights[EMBED_OUT]).astype(BF16)
        targets = dot(rows[:, DIM - 128 :], spread[...])
        names = (iota((GROUP * CAP, DIM), 1) + 512 * (me + 1)).astype(F32)
        pick = jnp.where((targets[:, :DIM] == names) | (targets[:, DIM:] == names), 1.0, 0.0).astype(BF16)
        preact = dot(grid_latent, weights[ENC_SEND]) + dot(pick, recv_proj[...])
        hidden = swish(preact).astype(BF16)
        hidden_sum[...] += dot_tn(pick, hidden)

    def received(group, count):
        block = arriving.at[pl.ds(group * GROUP, count)]
        pltpu.make_async_remote_copy(
            src_ref=block,
            dst_ref=block,
            send_sem=send_sem,
            recv_sem=recv_sem.at[group],
            device_id=(lat, lon),
            device_id_type=MESH,
        ).wait_recv()

    def whole_group(group, carry):
        received(group, GROUP)
        arrive(group)
        return carry

    lax.fori_loop(0, GROUPS - 1, whole_group, 0)
    own.wait()
    received(GROUPS - 1, GROUP - 1)
    arrive(GROUPS - 1)

    preact = self_part[...] + dot(hidden_sum[...].astype(BF16), fold_enc[...])
    hidden = swish(preact).astype(BF16)
    updated = (latent[...].astype(F32) + dot(hidden, weights[ENC_NODE_OUT])).astype(BF16)
    mesh_one[...] = updated
    projected[...] = dot(updated, weights[PROC_SEND]).astype(BF16)
    chosen_rows = dot(chooser[...], projected[...]).astype(BF16)
    halo_out[...] = chosen_rows.reshape(PEERS, HALO, DIM)
    for offset in OFFSETS:
        to_lat, to_lon = peer(offset)
        pltpu.make_async_remote_copy(
            src_ref=halo_out.at[to_lat * 16 + to_lon],
            dst_ref=halo_in.at[me],
            send_sem=halo_send_sem,
            recv_sem=halo_recv_sem,
            device_id=(to_lat, to_lon),
            device_id_type=MESH,
        ).start()
    own_halo = pltpu.make_async_copy(halo_out.at[me], halo_in.at[me], own_sem)
    own_halo.start()

    receiver[...] = dot(mesh_one[...], weights[PROC_RECV])

    def gather_local(k, carry):
        local_part[k] = dot(pick_local[k], projected[...]) + receiver[...]
        return carry

    lax.fori_loop(0, DEGREE, gather_local, 0)
    self_part[...] = dot(mesh_one[...], weights[PROC_NODE_SELF])

    own_halo.wait()
    halo_all = halo_in.at[pl.ds(0, PEERS - 1)]
    halo_wait = pltpu.make_async_remote_copy(
        src_ref=halo_all,
        dst_ref=halo_all,
        send_sem=halo_send_sem,
        recv_sem=halo_recv_sem,
        device_id=(lat, lon),
        device_id_type=MESH,
    )
    halo_wait.wait_recv()
    table = halo_in[...].reshape(PEERS * HALO, DIM)
    hidden_sum[...] = jnp.zeros((ROWS, DIM), F32)
    projected[...] = table

    def gather_halo(k, carry):
        hidden_sum[...] += swish(local_part[k] + dot(pick_halo[k], projected[...]))
        return carry

    lax.fori_loop(0, DEGREE, gather_halo, 0)
    preact = self_part[...] + dot(hidden_sum[...].astype(BF16), fold_proc[...])
    hidden = swish(preact).astype(BF16)
    out_ref[...] = (mesh_one[...].astype(F32) + dot(hidden, weights[PROC_NODE_OUT])).astype(BF16)

    halo_wait.wait_send()
    sent = arriving.at[pl.ds(0, PEERS - 1)]
    pltpu.make_async_remote_copy(
        src_ref=sent,
        dst_ref=sent,
        send_sem=send_sem,
        recv_sem=recv_sem.at[0],
        device_id=(lat, lon),
        device_id_type=MESH,
    ).wait_send()


def on_device(grid_feats, mesh_latent, embed_in, *rest):
    weights = rest[:13]
    dest_dev, dest_node, send_rows, src_slot = rest[13:]
    vmem = pltpu.VMEM
    square = vmem((DIM, DIM), BF16)
    scratch = [
        vmem((CHANNELS, ROWS), BF16),
        vmem((DIM, ROWS), BF16),
        square,
        vmem((CHANNELS, DIM), BF16),
        square,
        vmem((13, DIM, DIM), BF16),
        vmem((2, ROWS), jnp.int32),
        vmem((2, ROWS), jnp.int32),
        vmem((1, HALO, PEERS), jnp.int32),
        vmem((DEGREE, ROWS), jnp.int32),
        vmem((PEERS, CAP, DIM), BF16),
        vmem((PEERS, CAP, DIM), BF16),
        vmem((PEERS, HALO, DIM), BF16),
        vmem((PEERS, HALO, DIM), BF16),
        square,
        vmem((ROWS, DIM), F32),
        square,
        square,
        vmem((128, 2 * DIM), BF16),
        vmem((ROWS, DIM), F32),
        vmem((PEERS * HALO, ROWS), BF16),
        vmem((DEGREE, ROWS, ROWS), BF16),
        vmem((DEGREE, ROWS, PEERS * HALO), BF16),
        square,
        square,
        vmem((ROWS, DIM), F32),
        vmem((DEGREE, ROWS, DIM), F32),
        pltpu.SemaphoreType.DMA((7,)),
        pltpu.SemaphoreType.DMA((13,)),
        pltpu.SemaphoreType.DMA,
        pltpu.SemaphoreType.DMA((GROUPS,)),
        pltpu.SemaphoreType.DMA,
        pltpu.SemaphoreType.DMA,
        pltpu.SemaphoreType.DMA,
    ]
    return pl.pallas_call(
        kernel,
        out_shape=jax.ShapeDtypeStruct((ROWS, DIM), BF16),
        in_specs=[pl.BlockSpec(memory_space=pl.ANY)] * 20,
        out_specs=pl.BlockSpec(memory_space=pltpu.VMEM),
        scratch_shapes=scratch,
        compiler_params=pltpu.CompilerParams(
            collective_id=0, has_side_effects=True, vmem_limit_bytes=56 * 2**20
        ),
    )(
        grid_feats.T,
        mesh_latent,
        embed_in,
        *weights,
        dest_dev.T,
        dest_node.T,
        jnp.swapaxes(send_rows, 1, 2),
        src_slot.T,
    )


def solution(mesh):
    rows = P(("lat", "lon"), None)
    in_specs = (rows, rows, *([P()] * 14), rows, rows, P(("lat", "lon"), None, None), rows)
    return jax.shard_map(on_device, mesh=mesh, in_specs=in_specs, out_specs=rows, check_vma=False)
```

time: 158 us -> 57.6 us (0.36)
  matrix products: 77.6 us -> 0 us
  Pallas kernels: 0 us -> 55.6 us
  waiting for transfers between devices: 32.2 us -> 0 us
  blocking collectives: 20.8 us -> 0 us
  starting transfers between devices: 9.21 us -> 0 us
  other arithmetic: 8.99 us -> 0 us
  local copies, waits for them, and re-layouts: 7.79 us -> 1.87 us
    dot_general x26 -> x0, matrix products: 77.6 us -> none  [the longest x8 22.4 us: gather_block(): jnp.dot(pick, sender_table, preferred_element_type=jnp.float32)]
    pallas_call x0 -> x1, Pallas kernels: none -> 55.6 us  [on_device(): pl.pallas_call(kernel, out_shape=jax.ShapeDtypeStruct((ROWS, DIM), BF16),...]
    all_to_all x2 -> x0, waiting for transfers between devices: 32.2 us -> none  [the longest x1 21.7 us: on_device(): lax.all_to_all(payload.reshape(peer_count, capacity, -1), ('lat', 'lon'),...]
    all_to_all x1 -> x0, blocking collectives: 20.8 us -> none  [on_device(): lax.all_to_all(targets.reshape(peer_count, capacity), ('lat', 'lon'), spl...]
    all_to_all x2 -> x0, starting transfers between devices: 9.21 us -> none  [the longest x1 4.67 us: on_device(): lax.all_to_all(outgoing.reshape(peer_count, halo_count, latent_width), ('...]
    add x5 -> x0, other arithmetic: 2.77 us -> none  [the longest x4 2.76 us: fill_block(): columns = start + jnp.arange(slot_block, dtype=jnp.int32)]
    dynamic_slice x12 -> x0, local copies, waits for them, and re-layouts: 2.71 us -> none  [the longest x4 2.66 us: on_device(): payload_blocks, target_blocks = lax.map(fill_block, block_starts)]
    reduce_sum x5 -> x0, other arithmetic: 1.9 us -> none  [the longest x4 1.76 us: fill_block(): node_ids = jnp.sum(jnp.where(hits, dest_node[:, :, None], 0), axis=(0, 1))]
  transfers between devices with their start and end apart: 2 -> 0, of which waited for: 2 -> 0; matrix products, arithmetic and copies ran while one was open for 7% -> 0% of each run, Pallas kernels for 0% -> 0%
where the time goes in v1:
time: 57.6 us; the launch traced here: 57.5 us
  Pallas kernels  55.6 us (97%)
  local copies, waits for them, and re-layouts  1.87 us (3%)
    pallas_call x1, Pallas kernels, on_device(): pl.pallas_call(kernel, out_shape=jax.ShapeDtypeStruct((ROWS, DIM), BF16),...  55.6 us
    unnamed x1, local copies, waits for them, and re-layouts  1.87 us

profile of v1, /device:TPU:1, one launch (start us, length us, event | category | flops | bytes accessed | tf_op | source)
XLA Modules:
  0.0 57.5 jit_solution(2676472847801773392)
XLA Ops:
  0.0 55.6 %shard_map.190 = bf16[512,512]{1,0:T(8,128)(2,1)} custom-call(bf16[474,512]{1,0:T(8,128)(2,1)} %bitcast.5, bf16[512,512]{1,0:T(8,128)(2,1)} %latent_hbm.1, bf16[474,512]{1,0:T(8,128)(2,1)} %embed_in_hbm.1, bf16[512,512]{1,0:T(8,128)(2,1)} %rest_0_.1, bf16[512,512]{1,0:T(8,128)(2,1)} %rest_1_.1, bf16[512,512]{1,0:T(8,128)(2,1)} %rest_2_.1, ...), custom_call_target="tpu_custom_call" | custom-call | tf_op jit(solution)/shard_map/pallas_call | solution.py:395
  55.6 1.9 %copy.22 = bf16[512,512]{1,0:T(8,128)(2,1)} copy(bf16[512,512]{1,0:T(8,128)(2,1)} %shard_map.190) | data formatting | bytes 1048576

commit v2 on v1

--- a/solution.py
+++ b/solution.py
@@ -20,6 +20,7 @@
 ROWS = 512
 TAIL = CHANNELS // 16 * 16
 DEGREE = 8
+BLOCK = GROUP * CAP
 
 (
     EMBED_OUT,
@@ -57,6 +58,11 @@
 
 def swish(values):
     return values * (0.5 * jnp.tanh(0.5 * values) + 0.5)
+
+
+def swish_half(values):
+    half = (0.5 * values).astype(BF16)
+    return half * jnp.tanh(half) + half
 
 
 def dot(left, right):
@@ -102,7 +108,11 @@
         self_part,
         fold_enc,
         fold_proc,
-        spread,
+        sender_part,
+        names_out,
+        names_in,
+        pick_recv,
+        pick_node,
         hidden_sum,
         chooser,
         pick_local,
@@ -118,6 +128,7 @@
         halo_send_sem,
         halo_recv_sem,
         own_sem,
+        names_sem,
     ) = rest[18:]
 
     lat, lon = lax.axis_index("lat"), lax.axis_index("lon")
@@ -147,13 +158,15 @@
         pltpu.make_async_copy(source, weights.at[i], weight_sem.at[i])
         for i, source in enumerate(weights_hbm)
     ]
-    for load in loads:
+    for load in loads[:5]:
         load.start()
+    weight_loads[EMBED_OUT].start()
+    weight_loads[ENC_SEND].start()
 
     barrier = pltpu.get_barrier_semaphore()
     for offset in OFFSETS:
         pl.semaphore_signal(barrier, inc=1, device_id=peer(offset), device_id_type=MESH)
-    for load in weight_loads:
+    for load in weight_loads[ENC_RECV:] + loads[5:]:
         load.start()
 
     loads[0].wait()
@@ -162,40 +175,61 @@
     nodes = node[...]
     owner = iota((PEERS, ROWS), 0)
     hits = [dests[k : k + 1, :] == owner for k in range(2)]
-    onehot = jnp.concatenate([jnp.where(hit, 1.0, 0.0).astype(BF16) for hit in hits], axis=0)
+    onehot = [jnp.where(hit, 1.0, 0.0).astype(BF16) for hit in hits]
     earlier = jnp.where(iota((ROWS, ROWS), 0) < iota((ROWS, ROWS), 1), 1.0, 0.0).astype(BF16)
-    ranks = dot(onehot, earlier)
+    ranks = dot(jnp.concatenate(onehot, axis=0), earlier)
     first_count = jnp.sum(jnp.where(hits[0], 1.0, 0.0), axis=1, keepdims=True)
-    start = owner.astype(F32) * CAP
-    positions = [
-        jnp.sum(jnp.where(hits[0], ranks[:PEERS] + start, 0.0), axis=0, keepdims=True),
-        jnp.sum(jnp.where(hits[1], ranks[PEERS:] + first_count + start, 0.0), axis=0, keepdims=True),
+    ranks = [
+        jnp.sum(jnp.where(hits[0], ranks[:PEERS], 0.0), axis=0, keepdims=True).astype(jnp.int32),
+        jnp.sum(jnp.where(hits[1], ranks[PEERS:] + first_count, 0.0), axis=0, keepdims=True).astype(jnp.int32),
     ]
-    positions = [p.astype(jnp.int32) for p in positions]
-
-    loads[2].wait()
-    aug[0:TAIL, :] = feats[0:TAIL, :]
-    meta = [dests[0:1] + 1, nodes[0:1] // 32, nodes[0:1] % 32, dests[1:2] + 1, nodes[1:2] // 32, nodes[1:2] % 32]
+    positions = [dests[k : k + 1] * CAP + ranks[k] for k in range(2)]
+
+    named = jnp.zeros((PEERS, PEERS), F32)
+    for k in range(2):
+        at_slot = ranks[k] == iota((PEERS, ROWS), 0)
+        label = nodes[k : k + 1] + 1
+        for part in (label // 32 * 32, label % 32):
+            value = jnp.where(at_slot, part.astype(F32), 0.0).astype(BF16)
+            named += dot_nt(onehot[k], value)
+    names_out[...] = named.reshape(PEERS, 1, PEERS)
+
     left = CHANNELS - TAIL
-    tail = jnp.concatenate(
-        [feats[TAIL:CHANNELS, :].astype(F32), jnp.zeros((16 - left, ROWS), F32)], axis=0
-    )
-    tail_row = iota((16, ROWS), 0)
-    for i, value in enumerate(meta):
-        tail = jnp.where(tail_row == left + i, value.astype(F32), tail)
-    aug[TAIL : TAIL + 16, :] = tail.astype(BF16)
-    aug[TAIL + 16 :, :] = jnp.zeros((DIM - TAIL - 16, ROWS), BF16)
+    pad = jnp.zeros((16 - left, ROWS), F32)
+    rest_pad = jnp.zeros((DIM - TAIL - 16, DIM), BF16)
+    for load, raw, padded in ((loads[2], feats, aug), (loads[4], embed_raw, embed_in)):
+        load.wait()
+        padded[0:TAIL, :] = raw[0:TAIL, :]
+        padded[TAIL : TAIL + 16, :] = jnp.concatenate([raw[TAIL:CHANNELS, :].astype(F32), pad], axis=0).astype(BF16)
+        padded[TAIL + 16 :, :] = rest_pad
+    embedded = swish_half(dot_tn(aug[...], embed_in[...]))
+    weight_loads[EMBED_OUT].wait()
+    grid_latent = dot(embedded, weights[EMBED_OUT]).astype(BF16)
+    weight_loads[ENC_SEND].wait()
+    sender_part[...] = dot(grid_latent, weights[ENC_SEND]).astype(BF16)
 
     def pack(block, carry):
         slots = iota((512, ROWS), 0) + block * 512
         pick = jnp.where((positions[0] == slots) | (positions[1] == slots), 1.0, 0.0).astype(BF16)
-        rows = dot_nt(pick, aug[...]).astype(BF16)
+        rows = dot(pick, sender_part[...]).astype(BF16)
         outgoing[pl.ds(block * 32, 32)] = rows.reshape(32, CAP, DIM)
         return carry
 
     lax.fori_loop(0, PEERS * CAP // 512, pack, 0)
 
     pl.semaphore_wait(barrier, PEERS - 1)
+    for step, offset in enumerate(OFFSETS):
+        to_lat, to_lon = peer(offset)
+        pltpu.make_async_remote_copy(
+            src_ref=names_out.at[to_lat * 16 + to_lon],
+            dst_ref=names_in.at[step],
+            send_sem=names_sem.at[0],
+            recv_sem=names_sem.at[1],
+            device_id=(to_lat, to_lon),
+            device_id_type=MESH,
+        ).start()
+    own_names = pltpu.make_async_copy(names_out.at[me], names_in.at[PEERS - 1], names_sem.at[2])
+    own_names.start()
     for step, offset in enumerate(OFFSETS):
         to_lat, to_lon = peer(offset)
         pltpu.make_async_remote_copy(
@@ -209,24 +243,11 @@
     own = pltpu.make_async_copy(outgoing.at[me], arriving.at[PEERS - 1], own_sem)
     own.start()
 
-    loads[4].wait()
-    embed_in[0:TAIL, :] = embed_raw[0:TAIL, :]
-    embed_tail = jnp.concatenate(
-        [embed_raw[TAIL:CHANNELS, :].astype(F32), jnp.zeros((16 - left, DIM), F32)], axis=0
-    )
-    embed_in[TAIL : TAIL + 16, :] = embed_tail.astype(BF16)
-    embed_in[TAIL + 16 :, :] = jnp.zeros((DIM - TAIL - 16, DIM), BF16)
     loads[3].wait()
-    for load in weight_loads:
+    for load in weight_loads[ENC_RECV:]:
         load.wait()
     recv_proj[...] = dot(latent[...], weights[ENC_RECV]).astype(BF16)
     hidden_sum[...] = jnp.zeros((ROWS, DIM), F32)
-    lane = iota((128, 2 * DIM), 0) - (CHANNELS - (DIM - 128))
-    right = jnp.where(iota((128, 2 * DIM), 1) >= DIM, 3, 0)
-    lane = lane - right
-    spread[...] = jnp.where(
-        lane == 0, 512.0, jnp.where(lane == 1, 32.0, jnp.where(lane == 2, 1.0, 0.0))
-    ).astype(BF16)
     self_part[...] = dot(latent[...], weights[ENC_NODE_SELF])
     fold_enc[...] = dot(weights[ENC_EDGE_OUT], weights[ENC_NODE_AGG]).astype(BF16)
     fold_proc[...] = dot(weights[PROC_EDGE_OUT], weights[PROC_NODE_AGG]).astype(BF16)
@@ -254,16 +275,39 @@
         pick_local[k] = jnp.where(wanted == node_lane, 1.0, 0.0).astype(BF16)
         pick_halo[k] = jnp.where(wanted - ROWS == node_lane, 1.0, 0.0).astype(BF16)
 
+    own_names.wait()
+    names_all = names_in.at[pl.ds(0, PEERS - 1)]
+    names_wait = pltpu.make_async_remote_copy(
+        src_ref=names_all,
+        dst_ref=names_all,
+        send_sem=names_sem.at[0],
+        recv_sem=names_sem.at[1],
+        device_id=(lat, lon),
+        device_id_type=MESH,
+    )
+    names_wait.wait_recv()
+    labels = names_in[...].reshape(PEERS, PEERS).astype(jnp.int32)
+    parts = [part.astype(F32).astype(BF16) for part in (labels // 32 * 32, labels % 32)]
+    ones = jnp.ones((16, PEERS), BF16)
+
+    def prepare(block, carry):
+        first = block * BLOCK
+        expand = jnp.where((iota((BLOCK, PEERS), 0) + first) // CAP == iota((BLOCK, PEERS), 1), 1.0, 0.0).astype(BF16)
+        own_lane = iota((BLOCK, PEERS), 0) % CAP == iota((BLOCK, PEERS), 1)
+        spread = [jnp.where(own_lane, dot(expand, part), 0.0) for part in parts]
+        column = jnp.sum(spread[0] + spread[1], axis=1, keepdims=True).astype(jnp.int32) - 1
+        row = (dot_nt(ones, spread[0].astype(BF16)) + dot_nt(ones, spread[1].astype(BF16)))[0:1].astype(jnp.int32) - 1
+        pick = jnp.where(column == iota((BLOCK, ROWS), 1), 1.0, 0.0).astype(BF16)
+        pick_recv[block] = dot(pick, recv_proj[...]).astype(BF16)
+        pick_node[block] = jnp.where(row == iota((ROWS, BLOCK), 0), 1.0, 0.0).astype(BF16)
+        return carry
+
+    lax.fori_loop(0, PEERS * CAP // BLOCK, prepare, 0)
+
     def arrive(group):
         rows = arriving[pl.ds(group * GROUP, GROUP)].reshape(GROUP * CAP, DIM)
-        embedded = swish(dot(rows, embed_in[...])).astype(BF16)
-        grid_latent = dot(embedded, weights[EMBED_OUT]).astype(BF16)
-        targets = dot(rows[:, DIM - 128 :], spread[...])
-        names = (iota((GROUP * CAP, DIM), 1) + 512 * (me + 1)).astype(F32)
-        pick = jnp.where((targets[:, :DIM] == names) | (targets[:, DIM:] == names), 1.0, 0.0).astype(BF16)
-        preact = dot(grid_latent, weights[ENC_SEND]) + dot(pick, recv_proj[...])
-        hidden = swish(preact).astype(BF16)
-        hidden_sum[...] += dot_tn(pick, hidden)
+        hidden = swish_half(rows.astype(F32) + pick_recv[group].astype(F32))
+        hidden_sum[...] += dot(pick_node[group], hidden)
 
     def received(group, count):
         block = arriving.at[pl.ds(group * GROUP, count)]
@@ -276,12 +320,9 @@
             device_id_type=MESH,
         ).wait_recv()
 
-    def whole_group(group, carry):
+    for group in range(GROUPS - 1):
         received(group, GROUP)
         arrive(group)
-        return carry
-
-    lax.fori_loop(0, GROUPS - 1, whole_group, 0)
     own.wait()
     received(GROUPS - 1, GROUP - 1)
     arrive(GROUPS - 1)
@@ -330,15 +371,14 @@
     hidden_sum[...] = jnp.zeros((ROWS, DIM), F32)
     projected[...] = table
 
-    def gather_halo(k, carry):
-        hidden_sum[...] += swish(local_part[k] + dot(pick_halo[k], projected[...]))
-        return carry
-
-    lax.fori_loop(0, DEGREE, gather_halo, 0)
+    for k in range(DEGREE):
+        hidden_sum[...] += swish_half(local_part[k] + dot(pick_halo[k], projected[...])).astype(F32)
+
     preact = self_part[...] + dot(hidden_sum[...].astype(BF16), fold_proc[...])
     hidden = swish(preact).astype(BF16)
     out_ref[...] = (mesh_one[...].astype(F32) + dot(hidden, weights[PROC_NODE_OUT])).astype(BF16)
 
+    names_wait.wait_send()
     halo_wait.wait_send()
     sent = arriving.at[pl.ds(0, PEERS - 1)]
     pltpu.make_async_remote_copy(
@@ -375,7 +415,11 @@
         vmem((ROWS, DIM), F32),
         square,
         square,
-        vmem((128, 2 * DIM), BF16),
+        square,
+        vmem((PEERS, 1, PEERS), F32),
+        vmem((PEERS, 1, PEERS), F32),
+        vmem((GROUPS, BLOCK, DIM), BF16),
+        vmem((GROUPS, ROWS, BLOCK), BF16),
         vmem((ROWS, DIM), F32),
         vmem((PEERS * HALO, ROWS), BF16),
         vmem((DEGREE, ROWS, ROWS), BF16),
@@ -391,6 +435,7 @@
         pltpu.SemaphoreType.DMA,
         pltpu.SemaphoreType.DMA,
         pltpu.SemaphoreType.DMA,
+        pltpu.SemaphoreType.DMA((3,)),
     ]
     return pl.pallas_call(
         kernel,

time: 57.6 us -> 54.1 us (0.939)
  Pallas kernels: 55.6 us -> 52.1 us
    pallas_call x1, Pallas kernels: 55.6 us -> 52.1 us  [on_device(): pl.pallas_call(kernel, out_shape=jax.ShapeDtypeStruct((ROWS, DIM), BF16),...]
where the time goes in v2:
time: 54.1 us; the launch traced here: 54 us
  Pallas kernels  52.1 us (96%)
  local copies, waits for them, and re-layouts  1.87 us (3%)
    pallas_call x1, Pallas kernels, on_device(): pl.pallas_call(kernel, out_shape=jax.ShapeDtypeStruct((ROWS, DIM), BF16),...  52.1 us
    unnamed x1, local copies, waits for them, and re-layouts  1.87 us

profile of v2, /device:TPU:1, one launch (start us, length us, event | category | flops | bytes accessed | tf_op | source)
XLA Modules:
  0.0 54.0 jit_solution(7066178593710018309)
XLA Ops:
  0.0 52.1 %shard_map.190 = bf16[512,512]{1,0:T(8,128)(2,1)} custom-call(bf16[474,512]{1,0:T(8,128)(2,1)} %bitcast.5, bf16[512,512]{1,0:T(8,128)(2,1)} %latent_hbm.1, bf16[474,512]{1,0:T(8,128)(2,1)} %embed_in_hbm.1, bf16[512,512]{1,0:T(8,128)(2,1)} %rest_0_.1, bf16[512,512]{1,0:T(8,128)(2,1)} %rest_1_.1, bf16[512,512]{1,0:T(8,128)(2,1)} %rest_2_.1, ...), custom_call_target="tpu_custom_call" | custom-call | tf_op jit(solution)/shard_map/pallas_call | solution.py:440
  52.1 1.9 %copy.22 = bf16[512,512]{1,0:T(8,128)(2,1)} copy(bf16[512,512]{1,0:T(8,128)(2,1)} %shard_map.190) | data formatting | bytes 1048576

commit v3 on v2

--- a/solution.py
+++ b/solution.py
@@ -108,6 +108,7 @@
         self_part,
         fold_enc,
         fold_proc,
+        fold_send,
         sender_part,
         names_out,
         names_in,
@@ -250,6 +251,8 @@
     hidden_sum[...] = jnp.zeros((ROWS, DIM), F32)
     self_part[...] = dot(latent[...], weights[ENC_NODE_SELF])
     fold_enc[...] = dot(weights[ENC_EDGE_OUT], weights[ENC_NODE_AGG]).astype(BF16)
+    fold_send[...] = dot(weights[ENC_NODE_OUT], weights[PROC_SEND]).astype(BF16)
+    receiver[...] = dot(latent[...], weights[PROC_SEND])
     fold_proc[...] = dot(weights[PROC_EDGE_OUT], weights[PROC_NODE_AGG]).astype(BF16)
 
     loads[5].wait()
@@ -329,9 +332,7 @@
 
     preact = self_part[...] + dot(hidden_sum[...].astype(BF16), fold_enc[...])
     hidden = swish(preact).astype(BF16)
-    updated = (latent[...].astype(F32) + dot(hidden, weights[ENC_NODE_OUT])).astype(BF16)
-    mesh_one[...] = updated
-    projected[...] = dot(updated, weights[PROC_SEND]).astype(BF16)
+    projected[...] = (receiver[...] + dot(hidden, fold_send[...])).astype(BF16)
     chosen_rows = dot(chooser[...], projected[...]).astype(BF16)
     halo_out[...] = chosen_rows.reshape(PEERS, HALO, DIM)
     for offset in OFFSETS:
@@ -347,6 +348,7 @@
     own_halo = pltpu.make_async_copy(halo_out.at[me], halo_in.at[me], own_sem)
     own_halo.start()
 
+    mesh_one[...] = (latent[...].astype(F32) + dot(hidden, weights[ENC_NODE_OUT])).astype(BF16)
     receiver[...] = dot(mesh_one[...], weights[PROC_RECV])
 
     def gather_local(k, carry):
@@ -413,6 +415,7 @@
         vmem((PEERS, HALO, DIM), BF16),
         square,
         vmem((ROWS, DIM), F32),
+        square,
         square,
         square,
         square,

time: 54.1 us -> 53.8 us (level)
  no operation moved by 1% of the time
where the time goes in v3:
time: 53.8 us; the launch traced here: 53.7 us
  Pallas kernels  51.8 us (96%)
  local copies, waits for them, and re-layouts  1.87 us (3%)
    pallas_call x1, Pallas kernels, on_device(): pl.pallas_call(kernel, out_shape=jax.ShapeDtypeStruct((ROWS, DIM), BF16),...  51.8 us
    unnamed x1, local copies, waits for them, and re-layouts  1.87 us

profile of v3, /device:TPU:1, one launch (start us, length us, event | category | flops | bytes accessed | tf_op | source)
XLA Modules:
  0.0 53.7 jit_solution(2757057121286779174)
XLA Ops:
  0.0 51.8 %shard_map.190 = bf16[512,512]{1,0:T(8,128)(2,1)} custom-call(bf16[474,512]{1,0:T(8,128)(2,1)} %bitcast.5, bf16[512,512]{1,0:T(8,128)(2,1)} %latent_hbm.1, bf16[474,512]{1,0:T(8,128)(2,1)} %embed_in_hbm.1, bf16[512,512]{1,0:T(8,128)(2,1)} %rest_0_.1, bf16[512,512]{1,0:T(8,128)(2,1)} %rest_1_.1, bf16[512,512]{1,0:T(8,128)(2,1)} %rest_2_.1, ...), custom_call_target="tpu_custom_call" | custom-call | tf_op jit(solution)/shard_map/pallas_call | solution.py:443
  51.8 1.9 %copy.22 = bf16[512,512]{1,0:T(8,128)(2,1)} copy(bf16[512,512]{1,0:T(8,128)(2,1)} %shard_map.190) | data formatting | bytes 1048576

commit v4 on v3

--- a/solution.py
+++ b/solution.py
@@ -331,7 +331,7 @@
     arrive(GROUPS - 1)
 
     preact = self_part[...] + dot(hidden_sum[...].astype(BF16), fold_enc[...])
-    hidden = swish(preact).astype(BF16)
+    hidden = swish_half(preact)
     projected[...] = (receiver[...] + dot(hidden, fold_send[...])).astype(BF16)
     chosen_rows = dot(chooser[...], projected[...]).astype(BF16)
     halo_out[...] = chosen_rows.reshape(PEERS, HALO, DIM)
@@ -377,7 +377,7 @@
         hidden_sum[...] += swish_half(local_part[k] + dot(pick_halo[k], projected[...])).astype(F32)
 
     preact = self_part[...] + dot(hidden_sum[...].astype(BF16), fold_proc[...])
-    hidden = swish(preact).astype(BF16)
+    hidden = swish_half(preact)
     out_ref[...] = (mesh_one[...].astype(F32) + dot(hidden, weights[PROC_NODE_OUT])).astype(BF16)
 
     names_wait.wait_send()

time: 53.8 us -> 53.7 us (level)
  no operation moved by 1% of the time
where the time goes in v4:
time: 53.7 us; the launch traced here: 53.6 us
  Pallas kernels  51.7 us (96%)
  local copies, waits for them, and re-layouts  1.87 us (3%)
    pallas_call x1, Pallas kernels, on_device(): pl.pallas_call(kernel, out_shape=jax.ShapeDtypeStruct((ROWS, DIM), BF16),...  51.7 us
    unnamed x1, local copies, waits for them, and re-layouts  1.87 us

profile of v4, /device:TPU:1, one launch (start us, length us, event | category | flops | bytes accessed | tf_op | source)
XLA Modules:
  0.0 53.6 jit_solution(17929221559090264072)
XLA Ops:
  0.0 51.7 %shard_map.190 = bf16[512,512]{1,0:T(8,128)(2,1)} custom-call(bf16[474,512]{1,0:T(8,128)(2,1)} %bitcast.5, bf16[512,512]{1,0:T(8,128)(2,1)} %latent_hbm.1, bf16[474,512]{1,0:T(8,128)(2,1)} %embed_in_hbm.1, bf16[512,512]{1,0:T(8,128)(2,1)} %rest_0_.1, bf16[512,512]{1,0:T(8,128)(2,1)} %rest_1_.1, bf16[512,512]{1,0:T(8,128)(2,1)} %rest_2_.1, ...), custom_call_target="tpu_custom_call" | custom-call | tf_op jit(solution)/shard_map/pallas_call | solution.py:443
  51.7 1.9 %copy.22 = bf16[512,512]{1,0:T(8,128)(2,1)} copy(bf16[512,512]{1,0:T(8,128)(2,1)} %shard_map.190) | data formatting | bytes 1048576
